TPU v7x, 512 devices: a whole 4x8x8 slice. The times are simulated.
512 devices in a mesh: tm: 32 (over z, x_lo, core), space: 16 (over y, x_hi).
Axes of the slice: x: 4 (x_hi: 2, x_lo: 2; x = x_hi * 2 + x_lo), y: 8, z: 8, core: 2. Of those that a mesh axis runs over, the one named last changes fastest.
Arguments:
- snapshots: bfloat16 [16384, 49152], P('tm', 'space')
- freq_ids: int32 [64], replicated, may hold values from 0 to 127
Outputs:
- gram: float32 [64, 2, 63, 63], P('tm')
All inputs are finite; a program needn't handle non-finite values.
Results may differ from a plain program's by a relative error of at most 0.00039.
Values may be sent and summed in bfloat16 or wider, within the bound.
A program may use at most 64 MiB of HBM per device.

v0:
```python
import math

import jax
import jax.numpy as jnp
from jax import lax
from jax.sharding import PartitionSpec as P

NFFT = 512
F = 64


def shifted(block, axis, distance):
    devices = range(lax.axis_size(axis))
    route = [(i - distance, i) for i in devices if i - distance in devices]
    return lax.ppermute(block, axis, route)


def kernel_values(freqs, shifts, window_length):
    phase = freqs * shifts % window_length
    angle = 2.0 * math.pi / window_length * phase.astype(jnp.float32)
    window = 0.5 - 0.5 * jnp.cos(2.0 * math.pi / window_length * shifts.astype(jnp.float32))
    return (window * jnp.cos(angle), -window * jnp.sin(angle))


def local(snapshots, freq_ids):
    hop_len = NFFT // 2
    count_tm = lax.axis_size("tm")
    blocks = 2 * count_tm - 1
    device = lax.axis_index("tm")
    points = snapshots.shape[1]
    slot_ids = device * 2 - 1 + jnp.arange(3, dtype=jnp.int32)
    starts = hop_len * slot_ids
    shifts = device * NFFT + jnp.arange(NFFT, dtype=jnp.int32)[None, :] - starts[:, None]
    valid = (
        (shifts >= 0) & (shifts < NFFT) & (slot_ids[:, None] >= 0) & (slot_ids[:, None] < blocks)
    )
    clipped = jnp.where(valid, shifts, 0)
    real_part, imag_part = kernel_values(freq_ids[None, :, None], clipped[:, None, :], NFFT)
    kernel = jnp.stack([real_part, imag_part], axis=2)
    kernel = jnp.where(valid[:, None, None, :], kernel, 0.0).astype(jnp.bfloat16)
    kernel = kernel.reshape(6 * F, NFFT)
    partial_dft = jnp.dot(kernel, snapshots, preferred_element_type=jnp.float32).reshape(
        3, 2 * F, points
    )
    received = shifted(partial_dft[:1], "tm", -1)
    zero_padded_series = jnp.concatenate([jnp.zeros_like(received), received], axis=0)
    owned = (partial_dft[1:] + zero_padded_series).astype(jnp.bfloat16)
    owned = owned.reshape(2, F, 2, points)
    by_freq = lax.all_to_all(owned, "tm", split_axis=1, concat_axis=0, tiled=True)
    slots_all = by_freq.shape[0]
    resident_frequencies = by_freq.shape[1]
    stacked_snapshot_rows = jnp.transpose(by_freq, (1, 2, 0, 3)).reshape(
        resident_frequencies, 2 * slots_all, points
    )
    cross_product_terms = jnp.einsum(
        "tnf,tof->tno",
        stacked_snapshot_rows,
        stacked_snapshot_rows,
        preferred_element_type=jnp.float32,
    )
    gram_real_matrix = (
        cross_product_terms[:, :slots_all, :slots_all]
        + cross_product_terms[:, slots_all:, slots_all:]
    )
    imag_gram = (
        cross_product_terms[:, slots_all:, :slots_all]
        - cross_product_terms[:, :slots_all, slots_all:]
    )
    scale = 1.0 / (NFFT * points * lax.axis_size("space"))
    resident_gram_matrix = (
        jnp.stack([gram_real_matrix, imag_gram], axis=1)[:, :, :blocks, :blocks] * scale
    )
    return lax.psum(resident_gram_matrix, "space")


def solution(mesh):
    return jax.shard_map(
        local,
        mesh=mesh,
        in_specs=(P("tm", "space"), P()),
        out_specs=P("tm", None, None, None),
        check_vma=False,
    )
```

profile of v0, /device:TPU:2, one launch (start us, length us, event | category | flops | bytes accessed | tf_op | source)
XLA Modules:
  0.0 177.3 jit_solution(13179704445394800250)
XLA Ops:
  0.0 0.0 copy-start
  0.0 0.1 fusion.9
  0.1 0.1 subtract_select_fusion
  0.2 0.1 multiply_subtract_fusion
  0.3 2.6 %cosine_multiply_fusion = (bf16[3,64,1,512]{3,1,2,0:T(8,128)(2,1)S(1)}, bf16[3,64,1,512]{3,1,2,0:T(8,128)(2,1)S(1)}) fusion(s32[3,512]{1,0:T(4,128)S(1)} %subtract_select_fusion, s32[64]{0:T(128)} %param.3, f32[3,512]{1,0:T(4,128)S(1)} %get-tuple-element.9, f32[3,512]{1,0:T(4,128)S(1)} %get-tuple-element.10), kind=kLoop, calls=%fused_computation.13 | loop fusion | flops 1769472 | bytes 411904 | tf_op jit(solution)/shard_map/mul | solution.py:22
  3.0 0.1 fusion
  3.1 1.2 copy.11
  4.2 1.1 convert_element_type.38
  5.4 0.0 copy-done
  5.4 1.4 fusion.14
  6.8 0.1 slice_bitcast_fusion
  6.9 1.9 %collective-permute-start = (f32[1,128,3072]{2,1,0:T(8,128)S(1)}, f32[1,128,3072]{2,1,0:T(8,128)S(1)}, u32[]{:S(2)}, u32[]{:S(2)}) collective-permute-start(f32[1,128,3072]{2,1,0:T(8,128)S(1)} %slice_bitcast_fusion), channel_id=1, source_target_pairs={{16,0},{32,16},{48,32},{64,48},{80,64},{96,80},{112,96},{128,112},... | collective-permute-start | bytes 4718600 | tf_op jit(solution)/shard_map/ppermute | solution.py:15
  8.8 0.3 slice.36
  9.2 17.6 %collective-permute-done = f32[1,128,3072]{2,1,0:T(8,128)S(1)} collective-permute-done((f32[1,128,3072]{2,1,0:T(8,128)S(1)}, f32[1,128,3072]{2,1,0:T(8,128)S(1)}, u32[]{:S(2)}, u32[]{:S(2)}) %collective-permute-start) | collective-permute-done | bytes 1572896 | tf_op jit(solution)/shard_map/ppermute | solution.py:15
  26.8 1.5 add_convert_fusion
  28.2 4.5 %reshape.289 = bf16[2,64,2,3072]{3,2,1,0:T(2,128)(2,1)} reshape(bf16[2,128,3072]{2,1,0:T(8,128)(2,1)} %add_convert_fusion) | data formatting | bytes 3145728 | tf_op jit(solution)/shard_map/reshape | solution.py:48
  32.7 2.5 %copy.12 = bf16[2,64,2,3072]{3,2,0,1:T(2,128)(2,1)S(1)} copy(bf16[2,64,2,3072]{3,2,1,0:T(2,128)(2,1)} %reshape.289) | data formatting | bytes 3145728 | tf_op jit(solution)/shard_map/reshape | solution.py:48
  35.2 54.1 %all_to_all.18 = bf16[2,64,2,3072]{3,2,0,1:T(2,128)(2,1)S(1)} all-to-all(bf16[2,64,2,3072]{3,2,0,1:T(2,128)(2,1)S(1)} %copy.12), channel_id=1, replica_groups=mesh['tm'=32,'space'=16] {'tm'}, dimensions={1} | all-to-all | bytes 3145728 | tf_op jit(solution)/shard_map/all_to_all | solution.py:49
  89.3 2.4 %copy.13 = bf16[32,2,2,2,3072]{4,1,0,3,2:T(2,128)(2,1)} copy(bf16[32,2,2,2,3072]{4,3,1,2,0:T(2,128)(2,1)S(1)} %bitcast.21) | data formatting | bytes 3145728 | tf_op jit(solution)/shard_map/all_to_all | solution.py:49
  91.7 4.6 %all_to_all.16 = bf16[64,2,2,3072]{3,0,2,1:T(8,128)(2,1)} reshape(bf16[32,2,2,2,3072]{4,1,0,3,2:T(2,128)(2,1)} %copy.13) | data formatting | bytes 3145728 | tf_op jit(solution)/shard_map/all_to_all | solution.py:49
  96.3 2.4 %fusion.15 = f32[2,128,128]{2,1,0:T(8,128)S(1)} fusion(bf16[2,128,3072]{2,1,0:T(8,128)(2,1)} %bitcast.19), kind=kOutput, calls=%fused_computation.34 | convolution fusion | flops 201326592 | bytes 1703936 | tf_op jit(solution)/shard_map/tnf,tof->tno/dot_general | solution.py:55
  98.8 0.1 fusion.6
  98.9 77.6 %psum.7 = f32[2,2,63,63]{3,2,0,1:T(8,128)S(1)} all-reduce(f32[2,2,63,63]{3,2,0,1:T(8,128)S(1)} %fusion.4), channel_id=1, replica_groups=mesh['tm'=32,'space'=16] {'space'}, use_global_device_ids=true, to_apply=%region_0.1 | all-reduce | flops 15876 | bytes 127008 | tf_op jit(solution)/shard_map/psum | solution.py:73
  176.6 0.8 copy.14
  (4 shorter events, 0.0 us)
Async XLA Ops:
  0.0 5.4 %copy-start = (bf16[512,3072]{1,0:T(8,128)(2,1)S(1)}, bf16[512,3072]{1,0:T(8,128)(2,1)}, u32[]{:S(2)}) copy-start(bf16[512,3072]{1,0:T(8,128)(2,1)} %param.2) | copy-start | bytes 9437188
  6.9 19.8 %collective-permute-start = (f32[1,128,3072]{2,1,0:T(8,128)S(1)}, f32[1,128,3072]{2,1,0:T(8,128)S(1)}, u32[]{:S(2)}, u32[]{:S(2)}) collective-permute-start(f32[1,128,3072]{2,1,0:T(8,128)S(1)} %slice_bitcast_fusion), channel_id=1, source_target_pairs={{16,0},{32,16},{48,32},{64,48},{80,64},{96,80},{112,96},{128,112},... | collective-permute-start | bytes 4718600 | tf_op jit(solution)/shard_map/ppermute | solution.py:15
where the time goes:
time: 178 us; the launch traced here: 177 us
  blocking collectives  132 us (74%)
  waiting for transfers between devices  17.6 us (10%)
  local copies, waits for them, and re-layouts  17.5 us (10%)
  other arithmetic  4.6 us (3%)
  matrix products  3.83 us (2%)
  starting transfers between devices  1.92 us (1%)
    psum x1, blocking collectives, local(): return lax.psum(resident_gram_matrix, 'space')  77.6 us
    all_to_all x1, blocking collectives, local(): lax.all_to_all(owned, 'tm', split_axis=1, concat_axis=0, tiled=True)  54.1 us
    ppermute x1, waiting for transfers between devices, shifted(): return lax.ppermute(block, axis, route)  17.6 us
    all_to_all x2, local copies, waits for them, and re-layouts, local(): lax.all_to_all(owned, 'tm', split_axis=1, concat_axis=0, tiled=True)  7.01 us
    reshape x2, local copies, waits for them, and re-layouts, local(): owned = owned.reshape(2, F, 2, points)  6.98 us
  transfers between devices with their start and end apart: 1, of which 1 were waited for; matrix products, arithmetic and copies ran while one was open for 0% of the time, Pallas kernels for 0%

commit v1 on v0

v1 whole, which is shorter than its diff:
```python
import functools
import math

import jax
import jax.numpy as jnp
from jax import lax
from jax.experimental import pallas as pl
from jax.experimental.pallas import tpu as pltpu
from jax.sharding import PartitionSpec as P

NFFT = 512
HALF = NFFT // 2
MESH = pl.DeviceIdType.MESH
F32 = jnp.float32
BF16 = jnp.bfloat16

ROWS = 16
PARTS = 3


def cosine(m):
    b = jnp.abs(m - 256) - 128
    x = b.astype(F32) * (2.0 * math.pi / NFFT)
    s = x * x
    p = jnp.full_like(x, 1.0 / math.factorial(13))
    for k in (11, 9, 7, 5, 3, 1):
        p = p * s + (-1.0 if k % 4 == 3 else 1.0) / math.factorial(k)
    return x * p


def iota(shape, dim):
    return lax.broadcasted_iota(jnp.int32, shape, dim)


def basis(freqs, first, n_tm):
    rows = 8 * n_tm
    row = iota((rows, freqs.shape[1]), 0)
    column = iota((rows, freqs.shape[1]), 1)
    wanted = 2 * lax.rem(first + row // 8, n_tm) + (row // 2) % 2
    freq = jnp.sum(jnp.where(column == wanted, freqs, 0).astype(F32), axis=1, keepdims=True)
    freq = freq.astype(jnp.int32)
    row = iota((rows, 1), 0)
    phase = freq * iota((rows, HALF), 1) + 128 * (row % 2)
    return cosine(phase & (NFFT - 1)), 1.0 - 2.0 * (freq & 1).astype(F32), (row // 4) % 2


def kernel(
    n_tm, n_space, lanes, scale,
    freq_ref, x_hbm, out_ref,
    x, even_w, left_w, right_w, swap,
    even, give_left, give_right, keep_left, keep_right, got_left, got_right, odd_left, odd_right,
    recv, gram, mine, shares, total,
    x_sem, give_sem, got_sem, send_sem, recv_sem, space_send, space_recv,
):
    me = lax.axis_index("tm")
    spot = lax.axis_index("space")
    blocks = 2 * n_tm
    half = n_tm // 2
    width = 4 * lanes

    barrier = pltpu.get_barrier_semaphore()

    @pl.loop(1, n_tm)
    def _(r):
        pl.semaphore_signal(
            barrier, inc=1, device_id={"tm": lax.rem(me + r, n_tm)}, device_id_type=MESH
        )

    @pl.loop(1, n_space)
    def _(r):
        pl.semaphore_signal(
            barrier, inc=1, device_id={"space": lax.rem(spot + r, n_space)}, device_id_type=MESH
        )

    def load(part):
        columns = pl.ds(pl.multiple_of(part * width, width), width)
        return pltpu.make_async_copy(x_hbm.at[:, columns], x.at[part], x_sem.at[part])

    for part in range(PARTS):
        load(part).start()

    window = 0.5 * cosine(iota((1, HALF), 1))
    rising, falling = 0.5 - window, 0.5 + window
    freqs = freq_ref[...]
    wave, sign, which = basis(freqs, me, n_tm)
    for h in range(2):
        kept = (which == h).astype(F32)
        even_w[h, :, :HALF] = (wave * rising * kept).astype(BF16)
        late = (wave * falling * (sign * kept)).astype(BF16)
        even_w[h, :, HALF:] = late
        left_w[h] = late
    wave, sign, which = basis(freqs, me + 1, n_tm)
    for h in range(2):
        right_w[h] = (wave * rising * (which == h).astype(F32)).astype(BF16)

    side = ROWS * ROWS
    out_row, in_row = iota((side, side), 0), iota((side, side), 1)
    swap[...] = (in_row == (out_row % ROWS) * ROWS + out_row // ROWS).astype(F32).astype(BF16)

    def transform(part, weights, start, stop):
        halves = []
        for pair in range(2):
            acc = None
            for h in range(2):
                columns = slice((2 * pair + h) * lanes, (2 * pair + h + 1) * lanes)
                term = jnp.dot(
                    weights[h], x[part, start:stop, columns], preferred_element_type=F32
                )
                acc = term if acc is None else acc + term
            halves.append(acc.reshape(n_tm, 8, lanes))
        return jnp.concatenate(halves, axis=1)

    def to_right(part):
        return pltpu.make_async_remote_copy(
            src_ref=give_right.at[part], dst_ref=got_left.at[part],
            send_sem=give_sem.at[0, part], recv_sem=got_sem.at[0, part],
            device_id={"tm": lax.rem(me + 1, n_tm)}, device_id_type=MESH,
        )

    def to_left(part):
        return pltpu.make_async_remote_copy(
            src_ref=give_left.at[part], dst_ref=got_right.at[part],
            send_sem=give_sem.at[1, part], recv_sem=got_sem.at[1, part],
            device_id={"tm": lax.rem(me + n_tm - 1, n_tm)}, device_id_type=MESH,
        )

    def post(part, tile, block, r):
        pltpu.make_async_remote_copy(
            src_ref=tile, dst_ref=recv.at[part, block],
            send_sem=send_sem.at[part], recv_sem=recv_sem.at[part],
            device_id={"tm": lax.rem(me + r, n_tm)}, device_id_type=MESH,
        ).start()

    def place(part, tile, block):
        pltpu.make_async_copy(tile, recv.at[part, block], recv_sem.at[part]).start()

    after = 2 * me + 1
    before = lax.rem(2 * me + blocks - 1, blocks)

    @pl.loop(0, PARTS)
    def _(part):
        load(part).wait()
        partial = transform(part, left_w, 0, HALF)
        keep_left[part] = partial[:half]
        give_left[part] = partial[half:].astype(BF16)
        partial = transform(part, right_w, HALF, NFFT)
        give_right[part] = partial[:half].astype(BF16)
        keep_right[part] = partial[half:]

        @pl.when(part == 0)
        def _():
            pl.semaphore_wait(barrier, n_tm + n_space - 2)

        to_right(part).start()
        to_left(part).start()
        even[part] = transform(part, even_w, 0, NFFT).astype(BF16)
        place(part, even.at[part, 0], 2 * me)
        post(part, even.at[part, half], 2 * me, half)

        @pl.loop(1, half)
        def _(r):
            post(part, even.at[part, r], 2 * me, r)
            post(part, even.at[part, n_tm - r], 2 * me, n_tm - r)

    @pl.loop(0, PARTS)
    def _(part):
        to_right(part).wait_recv()
        odd_left[part] = (keep_left[part] + got_left[part].astype(F32)).astype(BF16)
        to_left(part).wait_recv()
        odd_right[part] = (keep_right[part] + got_right[part].astype(F32)).astype(BF16)
        place(part, odd_left.at[part, 0], before)
        place(part, odd_right.at[part, half - 1], after)

        @pl.loop(1, half)
        def _(r):
            post(part, odd_left.at[part, r], before, r)
            post(part, odd_right.at[part, half - 1 - r], after, n_tm - r)

    gram[...] = jnp.zeros_like(gram)

    @pl.loop(0, PARTS)
    def _(part):
        pltpu.make_async_copy(recv.at[part], recv.at[part], recv_sem.at[part]).wait()
        groups = []
        for g in range(blocks // ROWS):
            tiles = recv[part, g * ROWS : (g + 1) * ROWS].reshape(side, lanes)
            groups.append(jnp.dot(swap[...], tiles, preferred_element_type=F32).astype(BF16))
        for f in range(2):
            acc = gram[f]
            for q in range(4):
                rows = [
                    group[(4 * q + 2 * f + c) * ROWS : (4 * q + 2 * f + c + 1) * ROWS]
                    for c in range(2)
                    for group in groups
                ]
                rows = jnp.concatenate(rows, axis=0)
                acc = acc + lax.dot_general(
                    rows, rows, (((1,), (1,)), ((), ())), preferred_element_type=F32
                )
            gram[f] = acc

    for f in range(2):
        both = gram[f]
        top, bottom = both[:blocks], both[blocks:]
        real_side = iota(top.shape, 1) < blocks
        mine[f * blocks : (f + 1) * blocks, :] = jnp.where(real_side, top, -top) + jnp.concatenate(
            [bottom[:, blocks:], bottom[:, :blocks]], axis=1
        )

    share = 2 * blocks // n_space

    def rows_of(spot):
        return pl.ds(pl.multiple_of(spot * share, share), share)

    @pl.loop(1, n_space)
    def _(r):
        other = lax.rem(spot + r, n_space)
        pltpu.make_async_remote_copy(
            src_ref=mine.at[rows_of(other)], dst_ref=shares.at[spot],
            send_sem=space_send.at[0], recv_sem=space_recv.at[0],
            device_id={"space": other}, device_id_type=MESH,
        ).start()

    shares[spot] = mine[rows_of(spot), :]
    others = shares.at[pl.ds(0, n_space - 1)]
    pltpu.make_async_copy(others, others, space_recv.at[0]).wait()
    total[rows_of(spot), :] = jnp.sum(shares[...], axis=0) * scale

    @pl.loop(1, n_space)
    def _(r):
        pltpu.make_async_remote_copy(
            src_ref=total.at[rows_of(spot)], dst_ref=total.at[rows_of(spot)],
            send_sem=space_send.at[1], recv_sem=space_recv.at[1],
            device_id={"space": lax.rem(spot + r, n_space)}, device_id_type=MESH,
        ).start()

    for part in range(PARTS):
        to_right(part).wait_send()
        to_left(part).wait_send()
        sent = recv.at[part, pl.ds(0, blocks - 3)]
        pltpu.make_async_copy(sent, sent, send_sem.at[part]).wait()
    pltpu.make_async_copy(others, others, space_send.at[0]).wait()
    pltpu.make_async_copy(others, others, space_recv.at[1]).wait()
    out_ref[...] = total[...]
    pltpu.make_async_copy(others, others, space_send.at[1]).wait()


def local(snapshots, freq_ids):
    n_tm, n_space = lax.axis_size("tm"), lax.axis_size("space")
    points = snapshots.shape[1]
    lanes = points // (4 * PARTS)
    blocks, half, rows = 2 * n_tm, n_tm // 2, 8 * n_tm
    dma = pltpu.SemaphoreType.DMA
    out = pl.pallas_call(
        functools.partial(kernel, n_tm, n_space, lanes, 1.0 / (NFFT * points * n_space)),
        out_shape=jax.ShapeDtypeStruct((2 * blocks, 2 * blocks), F32),
        in_specs=[
            pl.BlockSpec(memory_space=pltpu.VMEM),
            pl.BlockSpec(memory_space=pl.ANY),
        ],
        out_specs=pl.BlockSpec(memory_space=pltpu.VMEM),
        scratch_shapes=[
            pltpu.VMEM((PARTS, NFFT, 4 * lanes), BF16),
            pltpu.VMEM((2, rows, NFFT), BF16),
            pltpu.VMEM((2, rows, HALF), BF16),
            pltpu.VMEM((2, rows, HALF), BF16),
            pltpu.VMEM((ROWS * ROWS, ROWS * ROWS), BF16),
            pltpu.VMEM((PARTS, n_tm, ROWS, lanes), BF16),
            pltpu.VMEM((PARTS, half, ROWS, lanes), BF16),
            pltpu.VMEM((PARTS, half, ROWS, lanes), BF16),
            pltpu.VMEM((PARTS, half, ROWS, lanes), F32),
            pltpu.VMEM((PARTS, half, ROWS, lanes), F32),
            pltpu.VMEM((PARTS, half, ROWS, lanes), BF16),
            pltpu.VMEM((PARTS, half, ROWS, lanes), BF16),
            pltpu.VMEM((PARTS, half, ROWS, lanes), BF16),
            pltpu.VMEM((PARTS, half, ROWS, lanes), BF16),
            pltpu.VMEM((PARTS, blocks, ROWS, lanes), BF16),
            pltpu.VMEM((2, 2 * blocks, 2 * blocks), F32),
            pltpu.VMEM((2 * blocks, 2 * blocks), F32),
            pltpu.VMEM((n_space, 2 * blocks // n_space, 2 * blocks), F32),
            pltpu.VMEM((2 * blocks, 2 * blocks), F32),
            dma((PARTS,)),
            dma((2, PARTS)),
            dma((2, PARTS)),
            dma((PARTS,)),
            dma((PARTS,)),
            dma((2,)),
            dma((2,)),
        ],
        compiler_params=pltpu.CompilerParams(
            collective_id=0, has_side_effects=True, vmem_limit_bytes=60 * 2**20
        ),
        name="spod",
    )(freq_ids.reshape(1, -1), snapshots)
    out = out.reshape(2, blocks, 2, blocks).transpose(0, 2, 1, 3)
    return out[:, :, : blocks - 1, : blocks - 1]


def solution(mesh):
    return jax.shard_map(
        local,
        mesh=mesh,
        in_specs=(P("tm", "space"), P()),
        out_specs=P("tm", None, None, None),
        check_vma=False,
    )
```

time: 178 us -> 71 us (0.40)
  the two profiles are of different devices: /device:TPU:2 before, /device:TPU:1 now
where the time goes in v1:
time: 71 us; the launch traced here: 70.8 us
  Pallas kernels  69.2 us (97%)
  local copies, waits for them, and re-layouts  1.63 us (2%)
    pallas_call x1, Pallas kernels, local(): pl.pallas_call(functools.partial(kernel, n_tm, n_space, lanes, 1.0 / (NFF...  69.2 us

profile of v1, /device:TPU:1, one launch (start us, length us, event | category | flops | bytes accessed | tf_op | source)
XLA Modules:
  0.0 70.8 jit_solution(191051225946688117)
XLA Ops:
  0.0 69.2 %spod.1 = f32[128,128]{1,0:T(8,128)} custom-call(s32[1,64]{1,0:T(1,128)} %bitcast.3, bf16[512,3072]{1,0:T(8,128)(2,1)} %x_hbm.1), custom_call_target="tpu_custom_call" | custom-call | tf_op jit(solution)/shard_map/spod/pallas_call | solution.py:254
  69.2 1.0 %reshape.7 = f32[2,64,2,64]{3,2,1,0:T(2,128)S(1)} reshape(f32[128,128]{1,0:T(8,128)} %spod.1) | data formatting | bytes 131072 | tf_op jit(solution)/shard_map/reshape | solution.py:295
  70.2 0.7 slice.4

commit v2 on v1

--- a/solution.py
+++ b/solution.py
@@ -44,13 +44,17 @@
     return cosine(phase & (NFFT - 1)), 1.0 - 2.0 * (freq & 1).astype(F32), (row // 4) % 2
 
 
+def far_first(k, n):
+    return n // 2 + jnp.where(k % 2 == 0, k // 2, -(k // 2))
+
+
 def kernel(
     n_tm, n_space, lanes, scale,
-    freq_ref, x_hbm, out_ref,
-    x, even_w, left_w, right_w, swap,
-    even, give_left, give_right, keep_left, keep_right, got_left, got_right, odd_left, odd_right,
+    freq_hbm, x_hbm, out_ref,
+    freq, x, even_w, left_w, right_w, swap,
+    even, give_left, give_right, keep_left, keep_right, got_left, got_right, odd,
     recv, gram, mine, shares, total,
-    x_sem, give_sem, got_sem, send_sem, recv_sem, space_send, space_recv,
+    freq_sem, x_sem, give_sem, got_sem, send_sem, recv_sem, space_send, space_recv,
 ):
     me = lax.axis_index("tm")
     spot = lax.axis_index("space")
@@ -61,27 +65,28 @@
     barrier = pltpu.get_barrier_semaphore()
 
     @pl.loop(1, n_tm)
-    def _(r):
-        pl.semaphore_signal(
-            barrier, inc=1, device_id={"tm": lax.rem(me + r, n_tm)}, device_id_type=MESH
-        )
+    def _(k):
+        other = lax.rem(me + far_first(k, n_tm), n_tm)
+        pl.semaphore_signal(barrier, inc=1, device_id={"tm": other}, device_id_type=MESH)
 
     @pl.loop(1, n_space)
-    def _(r):
-        pl.semaphore_signal(
-            barrier, inc=1, device_id={"space": lax.rem(spot + r, n_space)}, device_id_type=MESH
-        )
+    def _(k):
+        other = lax.rem(spot + far_first(k, n_space), n_space)
+        pl.semaphore_signal(barrier, inc=1, device_id={"space": other}, device_id_type=MESH)
 
     def load(part):
         columns = pl.ds(pl.multiple_of(part * width, width), width)
         return pltpu.make_async_copy(x_hbm.at[:, columns], x.at[part], x_sem.at[part])
 
+    load_freq = pltpu.make_async_copy(freq_hbm, freq, freq_sem.at[0])
+    load_freq.start()
     for part in range(PARTS):
         load(part).start()
 
     window = 0.5 * cosine(iota((1, HALF), 1))
     rising, falling = 0.5 - window, 0.5 + window
-    freqs = freq_ref[...]
+    load_freq.wait()
+    freqs = freq[...]
     wave, sign, which = basis(freqs, me, n_tm)
     for h in range(2):
         kept = (which == h).astype(F32)
@@ -134,8 +139,13 @@
     def place(part, tile, block):
         pltpu.make_async_copy(tile, recv.at[part, block], recv_sem.at[part]).start()
 
+    has_before, has_after = me > 0, me < n_tm - 1
+    zeros = jnp.zeros((ROWS, lanes), BF16)
+    for part in range(PARTS):
+        recv[part, blocks - 1] = zeros
+
     after = 2 * me + 1
-    before = lax.rem(2 * me + blocks - 1, blocks)
+    before = 2 * me - 1
 
     @pl.loop(0, PARTS)
     def _(part):
@@ -151,36 +161,60 @@
         def _():
             pl.semaphore_wait(barrier, n_tm + n_space - 2)
 
-        to_right(part).start()
-        to_left(part).start()
+
+        @pl.when(has_after)
+        def _():
+            to_right(part).start()
+
+        @pl.when(has_before)
+        def _():
+            to_left(part).start()
+
         even[part] = transform(part, even_w, 0, NFFT).astype(BF16)
         place(part, even.at[part, 0], 2 * me)
-        post(part, even.at[part, half], 2 * me, half)
-
-        @pl.loop(1, half)
-        def _(r):
-            post(part, even.at[part, r], 2 * me, r)
-            post(part, even.at[part, n_tm - r], 2 * me, n_tm - r)
+
+        @pl.loop(0, n_tm)
+        def _(k):
+            r = lax.rem(k + n_tm - me, n_tm)
+
+            @pl.when(r != 0)
+            def _():
+                post(part, even.at[part, r], 2 * me, r)
 
     @pl.loop(0, PARTS)
     def _(part):
-        to_right(part).wait_recv()
-        odd_left[part] = (keep_left[part] + got_left[part].astype(F32)).astype(BF16)
-        to_left(part).wait_recv()
-        odd_right[part] = (keep_right[part] + got_right[part].astype(F32)).astype(BF16)
-        place(part, odd_left.at[part, 0], before)
-        place(part, odd_right.at[part, half - 1], after)
-
-        @pl.loop(1, half)
-        def _(r):
-            post(part, odd_left.at[part, r], before, r)
-            post(part, odd_right.at[part, half - 1 - r], after, n_tm - r)
+        @pl.when(has_before)
+        def _():
+            to_right(part).wait_recv()
+            odd[part, :half] = (keep_left[part] + got_left[part].astype(F32)).astype(BF16)
+            place(part, odd.at[part, 0], before)
+
+        @pl.when(has_after)
+        def _():
+            to_left(part).wait_recv()
+            summed = (keep_right[part] + got_right[part].astype(F32)).astype(BF16)
+            odd[part, half + 1 :] = summed[: half - 1]
+            odd[part, half] = summed[half - 1]
+            place(part, odd.at[part, half], after)
+
+        @pl.loop(0, n_tm)
+        def _(k):
+            r = lax.rem(k + n_tm - me, n_tm)
+
+            @pl.when((r > 0) & (r < half) & has_before)
+            def _():
+                post(part, odd.at[part, r], before, r)
+
+            @pl.when((r > half) & has_after)
+            def _():
+                post(part, odd.at[part, r], after, r)
 
     gram[...] = jnp.zeros_like(gram)
 
     @pl.loop(0, PARTS)
     def _(part):
-        pltpu.make_async_copy(recv.at[part], recv.at[part], recv_sem.at[part]).wait()
+        arrived = recv.at[part, pl.ds(0, blocks - 1)]
+        pltpu.make_async_copy(arrived, arrived, recv_sem.at[part]).wait()
         groups = []
         for g in range(blocks // ROWS):
             tiles = recv[part, g * ROWS : (g + 1) * ROWS].reshape(side, lanes)
@@ -213,8 +247,8 @@
         return pl.ds(pl.multiple_of(spot * share, share), share)
 
     @pl.loop(1, n_space)
-    def _(r):
-        other = lax.rem(spot + r, n_space)
+    def _(k):
+        other = lax.rem(spot + far_first(k, n_space), n_space)
         pltpu.make_async_remote_copy(
             src_ref=mine.at[rows_of(other)], dst_ref=shares.at[spot],
             send_sem=space_send.at[0], recv_sem=space_recv.at[0],
@@ -227,21 +261,35 @@
     total[rows_of(spot), :] = jnp.sum(shares[...], axis=0) * scale
 
     @pl.loop(1, n_space)
-    def _(r):
+    def _(k):
+        other = lax.rem(spot + far_first(k, n_space), n_space)
         pltpu.make_async_remote_copy(
             src_ref=total.at[rows_of(spot)], dst_ref=total.at[rows_of(spot)],
             send_sem=space_send.at[1], recv_sem=space_recv.at[1],
-            device_id={"space": lax.rem(spot + r, n_space)}, device_id_type=MESH,
+            device_id={"space": other}, device_id_type=MESH,
         ).start()
 
     for part in range(PARTS):
-        to_right(part).wait_send()
-        to_left(part).wait_send()
-        sent = recv.at[part, pl.ds(0, blocks - 3)]
+        sent = recv.at[part, pl.ds(0, n_tm - 1)]
         pltpu.make_async_copy(sent, sent, send_sem.at[part]).wait()
+        sent = recv.at[part, pl.ds(0, half - 1)]
+
+        @pl.when(has_after)
+        def _():
+            to_right(part).wait_send()
+            pltpu.make_async_copy(sent, sent, send_sem.at[part]).wait()
+
+        @pl.when(has_before)
+        def _():
+            to_left(part).wait_send()
+            pltpu.make_async_copy(sent, sent, send_sem.at[part]).wait()
+
     pltpu.make_async_copy(others, others, space_send.at[0]).wait()
     pltpu.make_async_copy(others, others, space_recv.at[1]).wait()
-    out_ref[...] = total[...]
+    for f in range(2):
+        rows = total[f * blocks : (f + 1) * blocks, :]
+        out_ref[f, :, 0, :] = rows[: blocks - 1, : blocks - 1]
+        out_ref[f, :, 1, :] = rows[: blocks - 1, blocks : 2 * blocks - 1]
     pltpu.make_async_copy(others, others, space_send.at[1]).wait()
 
 
@@ -253,13 +301,14 @@
     dma = pltpu.SemaphoreType.DMA
     out = pl.pallas_call(
         functools.partial(kernel, n_tm, n_space, lanes, 1.0 / (NFFT * points * n_space)),
-        out_shape=jax.ShapeDtypeStruct((2 * blocks, 2 * blocks), F32),
+        out_shape=jax.ShapeDtypeStruct((2, blocks - 1, 2, blocks - 1), F32),
         in_specs=[
-            pl.BlockSpec(memory_space=pltpu.VMEM),
+            pl.BlockSpec(memory_space=pl.ANY),
             pl.BlockSpec(memory_space=pl.ANY),
         ],
         out_specs=pl.BlockSpec(memory_space=pltpu.VMEM),
         scratch_shapes=[
+            pltpu.VMEM((1, freq_ids.shape[0]), jnp.int32),
             pltpu.VMEM((PARTS, NFFT, 4 * lanes), BF16),
             pltpu.VMEM((2, rows, NFFT), BF16),
             pltpu.VMEM((2, rows, HALF), BF16),
@@ -272,13 +321,13 @@
             pltpu.VMEM((PARTS, half, ROWS, lanes), F32),
             pltpu.VMEM((PARTS, half, ROWS, lanes), BF16),
             pltpu.VMEM((PARTS, half, ROWS, lanes), BF16),
-            pltpu.VMEM((PARTS, half, ROWS, lanes), BF16),
-            pltpu.VMEM((PARTS, half, ROWS, lanes), BF16),
+            pltpu.VMEM((PARTS, n_tm, ROWS, lanes), BF16),
             pltpu.VMEM((PARTS, blocks, ROWS, lanes), BF16),
             pltpu.VMEM((2, 2 * blocks, 2 * blocks), F32),
             pltpu.VMEM((2 * blocks, 2 * blocks), F32),
             pltpu.VMEM((n_space, 2 * blocks // n_space, 2 * blocks), F32),
             pltpu.VMEM((2 * blocks, 2 * blocks), F32),
+            dma((1,)),
             dma((PARTS,)),
             dma((2, PARTS)),
             dma((2, PARTS)),
@@ -288,12 +337,14 @@
             dma((2,)),
         ],
         compiler_params=pltpu.CompilerParams(
-            collective_id=0, has_side_effects=True, vmem_limit_bytes=60 * 2**20
+            collective_id=0, has_side_effects=True, vmem_limit_bytes=48 * 2**20
         ),
         name="spod",
-    )(freq_ids.reshape(1, -1), snapshots)
-    out = out.reshape(2, blocks, 2, blocks).transpose(0, 2, 1, 3)
-    return out[:, :, : blocks - 1, : blocks - 1]
+    )(
+        pltpu.with_memory_space_constraint(freq_ids.reshape(1, -1), pltpu.HBM),
+        pltpu.with_memory_space_constraint(snapshots, pltpu.HBM),
+    )
+    return out.transpose(0, 2, 1, 3)
 
 
 def solution(mesh):

time: 71 us -> 67.4 us (0.949)
  the two profiles are of different devices: /device:TPU:1 before, /device:TPU:2 now
where the time goes in v2:
time: 67.4 us; the launch traced here: 67.3 us
  Pallas kernels  66.6 us (99%)
    pallas_call x1, Pallas kernels, local(): pl.pallas_call(functools.partial(kernel, n_tm, n_space, lanes, 1.0 / (NFF...  66.6 us

profile of v2, /device:TPU:2, one launch (start us, length us, event | category | flops | bytes accessed | tf_op | source)
XLA Modules:
  0.0 67.3 jit_solution(8347743086145642564)
XLA Ops:
  0.0 66.6 %spod.1 = f32[2,63,2,63]{3,2,1,0:T(2,128)S(1)} custom-call(s32[1,64]{1,0:T(1,128)} %bitcast.3, bf16[512,3072]{1,0:T(8,128)(2,1)} %x_hbm.1), custom_call_target="tpu_custom_call" | custom-call | tf_op jit(solution)/shard_map/spod/pallas_call | solution.py:302
  66.6 0.7 copy.4

commit v3 on v2

--- a/solution.py
+++ b/solution.py
@@ -15,7 +15,7 @@
 BF16 = jnp.bfloat16
 
 ROWS = 16
-PARTS = 3
+PARTS = 1
 
 
 def cosine(m):
@@ -64,16 +64,6 @@
 
     barrier = pltpu.get_barrier_semaphore()
 
-    @pl.loop(1, n_tm)
-    def _(k):
-        other = lax.rem(me + far_first(k, n_tm), n_tm)
-        pl.semaphore_signal(barrier, inc=1, device_id={"tm": other}, device_id_type=MESH)
-
-    @pl.loop(1, n_space)
-    def _(k):
-        other = lax.rem(spot + far_first(k, n_space), n_space)
-        pl.semaphore_signal(barrier, inc=1, device_id={"space": other}, device_id_type=MESH)
-
     def load(part):
         columns = pl.ds(pl.multiple_of(part * width, width), width)
         return pltpu.make_async_copy(x_hbm.at[:, columns], x.at[part], x_sem.at[part])
@@ -83,17 +73,29 @@
     for part in range(PARTS):
         load(part).start()
 
+    @pl.loop(1, n_tm, unroll=True)
+    def _(k):
+        other = lax.rem(me + far_first(k, n_tm), n_tm)
+        pl.semaphore_signal(barrier, inc=1, device_id={"tm": other}, device_id_type=MESH)
+
+    @pl.loop(1, n_space, unroll=True)
+    def _(k):
+        other = lax.rem(spot + far_first(k, n_space), n_space)
+        pl.semaphore_signal(barrier, inc=1, device_id={"space": other}, device_id_type=MESH)
+
+
     window = 0.5 * cosine(iota((1, HALF), 1))
     rising, falling = 0.5 - window, 0.5 + window
     load_freq.wait()
     freqs = freq[...]
-    wave, sign, which = basis(freqs, me, n_tm)
+    wave, sign, which = basis(freqs, 0, n_tm)
     for h in range(2):
         kept = (which == h).astype(F32)
         even_w[h, :, :HALF] = (wave * rising * kept).astype(BF16)
-        late = (wave * falling * (sign * kept)).astype(BF16)
-        even_w[h, :, HALF:] = late
-        left_w[h] = late
+        even_w[h, :, HALF:] = (wave * falling * (sign * kept)).astype(BF16)
+    wave, sign, which = basis(freqs, me, n_tm)
+    for h in range(2):
+        left_w[h] = (wave * falling * (sign * (which == h).astype(F32))).astype(BF16)
     wave, sign, which = basis(freqs, me + 1, n_tm)
     for h in range(2):
         right_w[h] = (wave * rising * (which == h).astype(F32)).astype(BF16)
@@ -102,17 +104,20 @@
     out_row, in_row = iota((side, side), 0), iota((side, side), 1)
     swap[...] = (in_row == (out_row % ROWS) * ROWS + out_row // ROWS).astype(F32).astype(BF16)
 
-    def transform(part, weights, start, stop):
+    def transform(part, weights, start, stop, owners=slice(None)):
+        first, last, _ = owners.indices(n_tm)
         halves = []
         for pair in range(2):
             acc = None
             for h in range(2):
                 columns = slice((2 * pair + h) * lanes, (2 * pair + h + 1) * lanes)
                 term = jnp.dot(
-                    weights[h], x[part, start:stop, columns], preferred_element_type=F32
+                    weights[h, 8 * first : 8 * last],
+                    x[part, start:stop, columns],
+                    preferred_element_type=F32,
                 )
                 acc = term if acc is None else acc + term
-            halves.append(acc.reshape(n_tm, 8, lanes))
+            halves.append(acc.reshape(last - first, 8, lanes))
         return jnp.concatenate(halves, axis=1)
 
     def to_right(part):
@@ -170,16 +175,19 @@
         def _():
             to_left(part).start()
 
-        even[part] = transform(part, even_w, 0, NFFT).astype(BF16)
-        place(part, even.at[part, 0], 2 * me)
-
-        @pl.loop(0, n_tm)
-        def _(k):
-            r = lax.rem(k + n_tm - me, n_tm)
-
-            @pl.when(r != 0)
-            def _():
-                post(part, even.at[part, r], 2 * me, r)
+        for first in range(0, n_tm, half):
+            owners = slice(first, first + half)
+            even[part, owners] = transform(part, even_w, 0, NFFT, owners).astype(BF16)
+
+            @pl.loop(first, first + half)
+            def _(k):
+                @pl.when(k == me)
+                def _():
+                    place(part, even.at[part, k], 2 * me)
+
+                @pl.when(k != me)
+                def _():
+                    post(part, even.at[part, k], 2 * me, lax.rem(k + n_tm - me, n_tm))
 
     @pl.loop(0, PARTS)
     def _(part):

time: 67.4 us -> 65.1 us (0.966)
  the two profiles are of different devices: /device:TPU:2 before, /device:TPU:194 now
where the time goes in v3:
time: 65.1 us; the launch traced here: 64.9 us
  Pallas kernels  64.3 us (99%)
    pallas_call x1, Pallas kernels, local(): pl.pallas_call(functools.partial(kernel, n_tm, n_space, lanes, 1.0 / (NFF...  64.3 us

profile of v3, /device:TPU:194, one launch (start us, length us, event | category | flops | bytes accessed | tf_op | source)
XLA Modules:
  0.0 64.9 jit_solution(1129085997709108794)
XLA Ops:
  0.0 64.3 %spod.1 = f32[2,63,2,63]{3,2,1,0:T(2,128)S(1)} custom-call(s32[1,64]{1,0:T(1,128)} %bitcast.3, bf16[512,3072]{1,0:T(8,128)(2,1)} %x_hbm.1), custom_call_target="tpu_custom_call" | custom-call | tf_op jit(solution)/shard_map/spod/pallas_call | solution.py:310
  64.3 0.7 %copy.4 = f32[2,2,63,63]{3,1,2,0:T(2,128)} copy(f32[2,2,63,63]{3,1,2,0:T(2,128)S(1)} %bitcast.2) | data formatting | bytes 127008

commit v4 on v3

--- a/solution.py
+++ b/solution.py
@@ -254,7 +254,7 @@
     def rows_of(spot):
         return pl.ds(pl.multiple_of(spot * share, share), share)
 
-    @pl.loop(1, n_space)
+    @pl.loop(1, n_space, unroll=True)
     def _(k):
         other = lax.rem(spot + far_first(k, n_space), n_space)
         pltpu.make_async_remote_copy(
@@ -268,7 +268,7 @@
     pltpu.make_async_copy(others, others, space_recv.at[0]).wait()
     total[rows_of(spot), :] = jnp.sum(shares[...], axis=0) * scale
 
-    @pl.loop(1, n_space)
+    @pl.loop(1, n_space, unroll=True)
     def _(k):
         other = lax.rem(spot + far_first(k, n_space), n_space)
         pltpu.make_async_remote_copy(

time: 65.1 us -> 65.1 us (level)
  no operation moved by 1% of the time
where the time goes in v4:
time: 65.1 us; the launch traced here: 64.9 us
  Pallas kernels  64.3 us (99%)
    pallas_call x1, Pallas kernels, local(): pl.pallas_call(functools.partial(kernel, n_tm, n_space, lanes, 1.0 / (NFF...  64.3 us

profile of v4, /device:TPU:194, one launch (start us, length us, event | category | flops | bytes accessed | tf_op | source)
XLA Modules:
  0.0 64.9 jit_solution(18309731187195329783)
XLA Ops:
  0.0 64.3 %spod.1 = f32[2,63,2,63]{3,2,1,0:T(2,128)S(1)} custom-call(s32[1,64]{1,0:T(1,128)} %bitcast.3, bf16[512,3072]{1,0:T(8,128)(2,1)} %x_hbm.1), custom_call_target="tpu_custom_call" | custom-call | tf_op jit(solution)/shard_map/spod/pallas_call | solution.py:310
  64.3 0.7 %copy.4 = f32[2,2,63,63]{3,1,2,0:T(2,128)} copy(f32[2,2,63,63]{3,1,2,0:T(2,128)S(1)} %bitcast.2) | data formatting | bytes 127008
